TPU v7x, 256 devices: a whole 4x4x8 slice. The times are simulated.
256 devices in a mesh: loop: 64 (over z, y_hi, x), rep: 4 (over y_lo, core).
Axes of the slice: x: 4, y: 4 (y_hi: 2, y_lo: 2; y = y_hi * 2 + y_lo), z: 8, core: 2. Of those that a mesh axis runs over, the one named last changes fastest.
Arguments:
- descriptors: bfloat16 [65536, 128], P('loop'), may hold values from -6 to 6
- ard_scales: float32 [128], replicated, may hold values from 0.079549514 to 0.35355338
- noise: float32 [65536], P('loop'), may hold values from 0.1 to 1
- probes: float32 [16, 65536], P(None, 'loop'), may hold values from -7 to 7, as said below
Outputs:
- solution: float32 [16, 65536], P(None, 'loop')
- residual: float32 [16, 65536], P(None, 'loop')
- direction: float32 [16, 65536], P(None, 'loop')
Inputs may be any that keep to these rules, and one draw needn't show every extreme that they name: `probes`: entries of order one.
All inputs are finite; a program needn't handle non-finite values.
Results may differ from a plain program's by a relative error of at most 0.014.
Values may be sent and summed in bfloat16 or wider, within the bound.
A program may use at most 64 MiB of HBM per device.

v0:
```python
import math

import jax
import jax.numpy as jnp
from jax import lax
from jax.sharding import PartitionSpec as P


def prepare(descriptors, ard_scales):
    values = descriptors.astype(jnp.float32)
    unit = values * lax.rsqrt(jnp.mean(values * values, axis=1, keepdims=True) + 1e-06)
    scaled = (unit * ard_scales[None, :]).astype(jnp.bfloat16)
    widened = scaled.astype(jnp.float32)
    sqnorm = jnp.sum(widened * widened, axis=1)
    return (scaled, sqnorm)


def cg_update(rhs, image, rhs_share, image_share):
    norm_local = jnp.sum(rhs_share * rhs_share, axis=1)
    curve_local = jnp.sum(rhs_share * image_share, axis=1)
    norm_old = lax.psum(norm_local, ("loop", "rep"))
    curve = lax.psum(curve_local, ("loop", "rep"))
    alpha = norm_old / curve
    residual = rhs - alpha[:, None] * image
    residual_share = rhs_share - alpha[:, None] * image_share
    norm_new = lax.psum(jnp.sum(residual_share * residual_share, axis=1), ("loop", "rep"))
    solution = alpha[:, None] * rhs
    direction = residual + (norm_new / norm_old)[:, None] * rhs
    return (solution, residual, direction)


def local(descriptors, ard_scales, noise, probes):
    local_rows = descriptors.shape[0]
    share_rows = local_rows // lax.axis_size("rep")
    offset = lax.axis_index("rep") * share_rows
    scaled, sqnorm = prepare(descriptors, ard_scales)
    vector = probes.astype(jnp.bfloat16)
    source_scaled = lax.dynamic_slice_in_dim(scaled, offset, share_rows, 0).T
    source_vector = lax.dynamic_slice_in_dim(vector, offset, share_rows, 1)
    initial = jnp.zeros((probes.shape[0], local_rows), jnp.float32)
    piece_scaled = lax.all_gather(source_scaled, "loop", axis=1, tiled=True)
    piece_vector = lax.all_gather(source_vector, "loop", axis=1, tiled=True)
    columns = piece_scaled.shape[1]
    width = math.gcd(columns, 512)

    def one_block(block_index, running):
        block_scaled = lax.dynamic_slice_in_dim(piece_scaled, block_index * width, width, 1)
        block_vector = lax.dynamic_slice_in_dim(piece_vector, block_index * width, width, 1)
        block_wide = block_scaled.astype(jnp.float32)
        block_norm = jnp.sum(block_wide * block_wide, axis=0)
        cross = lax.dot_general(
            block_scaled, scaled, (((0,), (1,)), ((), ())), preferred_element_type=jnp.float32
        )
        distance = jnp.maximum(block_norm[:, None] + sqnorm[None, :] - 2.0 * cross, 0.0)
        kernel = jnp.exp(-0.5 * distance).astype(jnp.bfloat16)
        return running + jnp.dot(block_vector, kernel, preferred_element_type=jnp.float32)

    partial_sum = lax.fori_loop(0, columns // width, one_block, initial)
    rhs_share = lax.dynamic_slice_in_dim(probes, offset, share_rows, 1)
    product = lax.psum(partial_sum, "rep")
    image = product + noise[None, :] * probes
    image_share = lax.dynamic_slice_in_dim(image, offset, share_rows, 1)
    return cg_update(probes, image, rhs_share, image_share)


def solution(mesh):
    return jax.shard_map(
        local,
        mesh=mesh,
        in_specs=(P("loop", None), P(), P("loop"), P(None, "loop")),
        out_specs=(P(None, "loop"), P(None, "loop"), P(None, "loop")),
        check_vma=False,
    )
```

profile of v0, /device:TPU:1, one launch (start us, length us, event | category | flops | bytes accessed | tf_op | source)
XLA Modules:
  0.0 483.0 jit_solution(1439793713647822058)
XLA Ops:
  7.2 1.2 fusion.12
  8.4 1.3 multiply_reduce_fusion.1
  11.2 160.9 %all_gather.6 = bf16[16,16384]{1,0:T(8,128)(2,1)S(1)} all-gather(bf16[16,256]{1,0:T(8,128)(2,1)S(1)} %dynamic-slice_convert_fusion), channel_id=1, replica_groups=mesh['loop'=64,'rep'=4] {'loop'}, dimensions={1}, use_global_device_ids=true | all-gather | bytes 532480 | tf_op jit(solution)/shard_map/all_gather | solution.py:42
  172.1 89.8 %while.14 = (s32[]{:T(128)}, f32[16,1024]{1,0:T(8,128)S(1)}, bf16[16,16384]{1,0:T(8,128)(2,1)S(1)}, bf16[128,16384]{0,1:T(8,128)(2,1)}, f32[1024]{0:T(1024)S(1)}...) while((s32[]{:T(128)}, f32[16,1024]{1,0:T(8,128)S(1)}, ...), condition=%wide.region_6.0_spmd.clone, body=%wide.region_4.6_spmd.clone.sunk | while | flops 154369536 | bytes 1205920 | solution.py:58
  172.1 0.9 constant_dynamic-slice_fusion.6
  173.2 1.7 fusion.22
  174.9 0.9 constant_dynamic-slice_fusion.6
  176.0 1.7 fusion.22
  178.8 1.7 fusion.22
  180.6 0.9 constant_dynamic-slice_fusion.6
  181.7 1.7 fusion.22
  183.4 0.9 constant_dynamic-slice_fusion.6
  184.5 1.7 fusion.22
  187.3 1.7 fusion.22
  189.0 0.9 constant_dynamic-slice_fusion.6
  190.1 1.7 fusion.22
  191.8 0.9 constant_dynamic-slice_fusion.6
  192.9 1.7 fusion.22
  194.6 0.9 constant_dynamic-slice_fusion.6
  195.7 1.7 fusion.22
  197.4 0.9 constant_dynamic-slice_fusion.6
  198.5 1.7 fusion.22
  200.2 0.9 constant_dynamic-slice_fusion.6
  201.3 1.7 fusion.22
  204.1 1.7 fusion.22
  206.9 1.7 fusion.22
  209.7 1.7 fusion.22
  212.5 1.7 fusion.22
  215.3 1.7 fusion.22
  218.1 1.7 fusion.22
  220.9 1.7 fusion.22
  223.7 1.7 fusion.22
  226.5 1.7 fusion.22
  229.3 1.7 fusion.22
  232.2 1.7 fusion.22
  235.0 1.7 fusion.22
  237.8 1.7 fusion.22
  240.6 1.7 fusion.22
  243.4 1.7 fusion.22
  246.2 1.7 fusion.22
  249.0 1.7 fusion.22
  251.8 1.7 fusion.22
  254.6 1.7 fusion.22
  257.4 1.7 fusion.22
  260.2 1.7 fusion.22
  262.6 61.1 %all-reduce.3.cloned.1.call-done = f32[16,1024]{1,0:T(8,128)} async-done(((f32[16,1024]{1,0:T(8,128)}), f32[16,1024]{1,0:T(8,128)}) %all-reduce.3.cloned.1.call-update) | async-done | bytes 65552 | tf_op jit(solution)/shard_map/psum | solution.py:60
  324.6 77.0 %all-reduce = (f32[16]{0:T(128)S(1)}, f32[16]{0:T(128)S(1)}) all-reduce(f32[16]{0:T(128)S(1)} %get-tuple-element.141, f32[16]{0:T(128)S(1)} %get-tuple-element.140), channel_id=1, replica_groups=mesh['loop'=64,'rep'=4] {'loop','rep'}, use_global_device_ids=true, to_apply=%region_1.0 | all-reduce | flops 32 | bytes 256 | tf_op jit(solution)/shard_map/psum | solution.py:21
  401.9 73.6 %psum.31 = f32[16]{0:T(128)S(1)} all-reduce(f32[16]{0:T(128)S(1)} %multiply_reduce_fusion.2), channel_id=1, replica_groups=mesh['loop'=64,'rep'=4] {'loop','rep'}, use_global_device_ids=true, to_apply=%region_11.0 | all-reduce | flops 16 | bytes 128 | tf_op jit(solution)/shard_map/psum | solution.py:26
  (108 shorter events, 30.4 us)
Async XLA Ops:
  7.2 164.9 %all-gather.2.cloned.1.call-start = ((), (), s32[]{:S(2)}) async-start(), calls=%async_computation | async-start | bytes 4259840 | tf_op jit(solution)/shard_map/all_gather | solution.py:41
  10.4 313.3 %all-reduce.3.cloned.1.call-start = ((), (), s32[]{:S(2)}) async-start(), calls=%async_computation.1 | async-start | bytes 131072 | tf_op jit(solution)/shard_map/psum | solution.py:60
  172.1 151.6 %copy-start = (f32[16,1024]{1,0:T(8,128)S(1)}, f32[16,1024]{1,0:T(8,128)}, u32[]{:S(2)}) copy-start(f32[16,1024]{1,0:T(8,128)} %param.9) | copy-start | bytes 196612
  172.1 151.6 %copy-start.2 = (f32[1024]{0:T(1024)S(1)}, f32[1024]{0:T(1024)}, u32[]{:S(2)}) copy-start(f32[1024]{0:T(1024)} %param.8) | copy-start | bytes 12292
  261.9 0.6 copy-start.1
Sparse Core Ops, SparseCore 0:
  12.2 128.6 all-gather.1
  262.7 60.9 all-reduce.2
where the time goes:
time: 485 us; the launch traced here: 483 us
  blocking collectives  312 us (64%)
  waiting for transfers between devices  61.1 us (13%)
  matrix products  54.7 us (11%)
  local copies, waits for them, and re-layouts  35.1 us (7%)
  between operations  14.1 us (3%)
  other arithmetic  5.96 us (1%)
    all_gather x1, blocking collectives, local(): piece_vector = lax.all_gather(source_vector, 'loop', axis=1, tiled=True)  161 us
    psum x1, blocking collectives, cg_update(): norm_old = lax.psum(norm_local, ('loop', 'rep'))  77 us
    psum x1, blocking collectives, cg_update(): lax.psum(jnp.sum(residual_share * residual_share, axis=1), ('loop', 'rep'))  73.6 us
    psum x1, waiting for transfers between devices, local(): product = lax.psum(partial_sum, 'rep')  61.1 us
    dot_general x32, matrix products, one_block(): jnp.dot(block_vector, kernel, preferred_element_type=jnp.float32)  54.7 us
    dynamic_slice x64, local copies, waits for them, and re-layouts, one_block(): lax.dynamic_slice_in_dim(piece_scaled, block_index * width, width, 1)  33.1 us
  transfers between devices with their start and end apart: 2, of which 1 were waited for; matrix products, arithmetic and copies ran while one was open for 0% of the time, Pallas kernels for 0%

commit v1 on v0

v1 whole, which is shorter than its diff:
```python
import functools

import jax
import jax.numpy as jnp
from jax import lax
from jax.experimental import pallas as pl
from jax.experimental.pallas import tpu as pltpu
from jax.sharding import PartitionSpec as P

MESH = pl.DeviceIdType.MESH
F32 = jnp.float32
BF16 = jnp.bfloat16

FEAT = 128
AUG = 16
PROBES = 16
SHARD = 1024
HALF = 512
QUART = 256
DEEP = FEAT + AUG
PACK = FEAT + AUG + PROBES

GROUPS = (
    ((0, 0), (-1, 0), (1, 0), (0, 1)),
    ((-2, 0), (2, 0), (-1, 1), (1, 1)),
    ((-3, 0), (3, 0), (-2, 1), (2, 1)),
    ((4, 0), (-3, 1), (3, 1), (4, 1)),
)
PLACE = {piece: (g, i) for g, group in enumerate(GROUPS) for i, piece in enumerate(group)}
UP = {(0, 0): (-1, 0), (-1, 0): (-2, 0), (-2, 0): (-3, 0), (-3, 0): (4, 0), (-2, 1): (-3, 1)}
DOWN = {(0, 0): (1, 0), (1, 0): (2, 0), (2, 0): (3, 0), (2, 1): (3, 1), (3, 1): (4, 1)}
ACROSS = {(0, 0): (0, 1), (-1, 0): (-1, 1), (1, 0): (1, 1), (-2, 0): (-2, 1), (2, 0): (2, 1)}
TARGET_X = (0, 1, 3, 2)


def partners():
    found = set()
    for dz in range(1, 8):
        found.add((0, 0, 0, dz, 0))
    for dx in range(4):
        for flip in range(2):
            for dc in range(2):
                found.add((dx, flip, flip, 0, dc))
            found.add((dx, 0, flip, 0, 0))
    found.discard((0, 0, 0, 0, 0))
    return sorted(found)


def kernel(
    desc_ref, ard_ref, noise_ref, probes_ref, image_ref, scalars_ref,
    sbuf, tbuf, acc, reduced, stats, sums1, sums2,
    ring_send, core_send, t_send, r_send, i_send, s1_send, s2_send,
    ring_recv, core_recv, t_recv, r_recv, i_recv, s1_recv, s2_recv,
):
    loop = lax.axis_index("loop")
    rep = lax.axis_index("rep")
    z, yh, x = loop // 8, (loop // 4) % 2, loop % 4
    yl, c = rep // 2, rep % 2

    def device(dx=0, dh=0, dl=0, dz=0, dc=0):
        nz = (z + dz) % 8
        nh = (yh + dh) % 2
        nx = (x + dx) % 4
        nl = (yl + dl) % 2
        nc = (c + dc) % 2
        return (nz * 8 + nh * 4 + nx, nl * 2 + nc)

    barrier = pltpu.get_barrier_semaphore()
    greeted = partners()
    for offsets in greeted:
        pl.semaphore_signal(barrier, inc=1, device_id=device(*offsets), device_id_type=MESH)

    half_at = pl.multiple_of(c * HALF, HALF)
    share = (yl + yh) % 2
    source_at = pl.multiple_of(share * HALF + c * QUART, QUART)

    def prepare(rows):
        values = rows.astype(F32)
        mean = jnp.mean(values * values, axis=1, keepdims=True)
        unit = values * lax.rsqrt(mean + 1e-06)
        scaled = (unit * ard_ref[...]).astype(BF16)
        turned = scaled.astype(F32).T
        norm = -0.5 * jnp.sum(turned * turned, axis=0, keepdims=True)
        high = norm.astype(BF16).astype(F32)
        rest = norm - high
        mid = rest.astype(BF16).astype(F32)
        low = rest - mid
        return turned.astype(BF16), (high, mid, low)

    def extra(parts, first):
        count = parts[0].shape[1]
        row = lax.broadcasted_iota(jnp.int32, (AUG, count), 0)
        ones = 3 - first
        out = jnp.where((row >= ones) & (row < ones + 3), 1.0, 0.0)
        for n, part in enumerate(parts):
            out = jnp.where(row == first + n, part, out)
        return out.astype(BF16)

    def own(i):
        return pl.ds(pl.multiple_of(i * HALF + c * QUART, QUART), QUART)

    turned, parts = prepare(desc_ref[pl.ds(source_at, QUART), :])
    sbuf[0, 0:FEAT, own(0)] = turned
    sbuf[0, FEAT:DEEP, own(0)] = extra(parts, 0)
    sbuf[0, DEEP:PACK, own(0)] = probes_ref[:, pl.ds(source_at, QUART)].astype(BF16)
    turned, parts = prepare(desc_ref[pl.ds(half_at, HALF), :])
    tbuf[0, 0:FEAT, :] = turned
    tbuf[0, FEAT:DEEP, :] = extra(parts, 3)

    pl.semaphore_wait(barrier, len(greeted))

    started = {}

    def begin(key, make):
        make().start()
        started[key] = make

    def copy(src, dst, send, recv, to):
        return pltpu.make_async_remote_copy(
            src_ref=src, dst_ref=dst, send_sem=send, recv_sem=recv, device_id=to, device_id_type=MESH
        )

    def ring(src, dst, to):
        (g, i), (h, j) = PLACE[src], PLACE[dst]
        return copy(
            sbuf.at[g, :, own(i)], sbuf.at[h, :, own(j)], ring_send.at[h, j], ring_recv.at[h, j], to
        )

    def to_core(piece):
        g, i = PLACE[piece]
        return copy(
            sbuf.at[g, :, own(i)], sbuf.at[g, :, own(i)], core_send.at[g, i], core_recv.at[g, i], sibling
        )

    def from_core(piece):
        g, i = PLACE[piece]
        there = pl.ds(pl.multiple_of(i * HALF + (1 - c) * QUART, QUART), QUART)
        return copy(
            sbuf.at[g, :, there], sbuf.at[g, :, there], core_send.at[g, i], core_recv.at[g, i], sibling
        )

    ways = ((UP, device(dz=1)), (DOWN, device(dz=7)), (ACROSS, device(dh=1, dl=1)))
    sibling = device(dc=1)

    def forward(piece):
        for table, to in ways:
            if piece in table:
                begin(("ring", table[piece]), functools.partial(ring, piece, table[piece], to))
        begin(("core", piece), functools.partial(to_core, piece))

    def arrive(piece):
        ring(piece, piece, device(dz=1)).wait_recv()
        forward(piece)

    def target_copy(t):
        return copy(
            tbuf.at[0], tbuf.at[t], t_send.at[t], t_recv.at[t], device(dx=(4 - TARGET_X[t]) % 4)
        )

    forward((0, 0))
    for t in (1, 2, 3):
        begin(("t", t), functools.partial(target_copy, t))

    acc[...] = jnp.zeros_like(acc)

    def block(g, t):
        cross = lax.dot_general(
            sbuf[g, 0:DEEP, :], tbuf[t], (((0,), (0,)), ((), ())), preferred_element_type=F32
        )
        weights = jnp.exp(jnp.minimum(cross, 0.0)).astype(BF16)
        acc[t] += jnp.dot(sbuf[g, DEEP:PACK, :], weights, preferred_element_type=F32)

    for piece in GROUPS[0][1:]:
        arrive(piece)
    for piece in GROUPS[0]:
        from_core(piece).wait_recv()

    def body0(t, carry):
        for n in (1, 2, 3):
            @pl.when(t == n)
            def _(n=n):
                target_copy(n).wait_recv()
                if n == 3:
                    for piece in GROUPS[1]:
                        arrive(piece)
        block(0, t)
        return carry

    lax.fori_loop(0, 4, body0, 0)
    for piece in GROUPS[1]:
        from_core(piece).wait_recv()

    def body1(t, carry):
        @pl.when(t == 3)
        def _():
            for piece in GROUPS[2]:
                arrive(piece)
        block(1, t)
        return carry

    lax.fori_loop(0, 4, body1, 0)
    for piece in GROUPS[2]:
        from_core(piece).wait_recv()

    def body2(t, carry):
        @pl.when(t == 2)
        def _():
            for piece in ((3, 1), (4, 0), (-3, 1)):
                arrive(piece)
        @pl.when(t == 3)
        def _():
            arrive((4, 1))
        block(2, t)
        return carry

    lax.fori_loop(0, 4, body2, 0)
    for piece in GROUPS[3]:
        from_core(piece).wait_recv()

    mine = x * 2 + yl

    def reduce_copy(t, dl):
        dx = TARGET_X[t]
        return copy(
            acc.at[t], reduced.at[mine], r_send.at[t, dl], r_recv.at[mine], device(dx=dx, dl=dl)
        )

    def body3(n, carry):
        t = 3 - n
        block(3, t)
        for s in (3, 2, 1, 0):
            @pl.when(t == s)
            def _(s=s):
                for dl in (1, 0) if s else (1,):
                    begin(("r", s, dl), functools.partial(reduce_copy, s, dl))
        return carry

    lax.fori_loop(0, 4, body3, 0)
    reduced[mine] = acc[0]
    for t in (0, 1, 2, 3):
        for dl in (1, 0) if t else (1,):
            other = ((x + TARGET_X[t]) % 4) * 2 + (yl + dl) % 2
            copy(
                acc.at[t], reduced.at[other], r_send.at[t, dl], r_recv.at[other], device(dx=TARGET_X[t], dl=dl)
            ).wait_recv()

    total = reduced[0]
    for n in range(1, 8):
        total = total + reduced[n]
    rhs = probes_ref[:, pl.ds(half_at, HALF)]
    image = total + noise_ref[:, pl.ds(half_at, HALF)] * rhs
    norm = jnp.sum(rhs * rhs, axis=1, keepdims=True)
    curve = jnp.sum(rhs * image, axis=1, keepdims=True)
    square = jnp.sum(image * image, axis=1, keepdims=True)
    lane = lax.broadcasted_iota(jnp.int32, (PROBES, 128), 1)
    packed = jnp.where(lane == 0, norm, jnp.where(lane == 1, curve, square))
    here = x * 4 + yh * 2 + c
    sums1[here] = packed
    peers = [(dx, flip, dc) for dx in range(4) for flip in range(2) for dc in range(2)][1:]
    for n, (dx, flip, dc) in enumerate(peers):
        begin(("s1", n), functools.partial(
            copy, sums1.at[here], sums1.at[here], s1_send.at[n], s1_recv.at[here],
            device(dx=dx, dh=flip, dl=flip, dc=dc),
        ))
    image_ref[:, pl.ds(half_at, HALF)] = image
    span = pl.ds(half_at, HALF)
    other_span = pl.ds(pl.multiple_of((1 - c) * HALF, HALF), HALF)
    begin("image", functools.partial(
        copy, image_ref.at[:, span], image_ref.at[:, span], i_send.at[0], i_recv.at[0], device(dc=1)
    ))
    for n, (dx, flip, dc) in enumerate(peers):
        there = ((x + dx) % 4) * 4 + ((yh + flip) % 2) * 2 + (c + dc) % 2
        copy(
            sums1.at[there], sums1.at[there], s1_send.at[n], s1_recv.at[there],
            device(dx=dx, dh=flip, dl=flip, dc=dc),
        ).wait_recv()
    whole = sums1[0]
    for n in range(1, 16):
        whole = whole + sums1[n]
    sums2[z] = whole
    for dz in range(1, 8):
        begin(("s2", dz), functools.partial(
            copy, sums2.at[z], sums2.at[z], s2_send.at[dz - 1], s2_recv.at[z], device(dz=dz)
        ))
    for dz in range(1, 8):
        there = (z + dz) % 8
        copy(sums2.at[there], sums2.at[there], s2_send.at[dz - 1], s2_recv.at[there], device(dz=dz)).wait_recv()
    whole = sums2[0]
    for n in range(1, 8):
        whole = whole + sums2[n]
    norm, curve, square = whole[:, 0:1], whole[:, 1:2], whole[:, 2:3]
    alpha = norm / curve
    fresh = jnp.maximum(alpha * alpha * square - norm, 0.0)
    scalars_ref[...] = jnp.where(lane == 0, alpha, fresh / norm)
    copy(
        image_ref.at[:, other_span], image_ref.at[:, other_span], i_send.at[0], i_recv.at[0], device(dc=1)
    ).wait_recv()
    for make in started.values():
        make().wait_send()


def local(descriptors, ard_scales, noise, probes):
    dma = pltpu.SemaphoreType.DMA
    vmem = pl.BlockSpec(memory_space=pltpu.VMEM)
    image, scalars = pl.pallas_call(
        kernel,
        out_shape=(
            jax.ShapeDtypeStruct((PROBES, SHARD), F32),
            jax.ShapeDtypeStruct((PROBES, 128), F32),
        ),
        in_specs=[vmem] * 4,
        out_specs=(vmem, vmem),
        scratch_shapes=[
            pltpu.VMEM((4, PACK, 4 * HALF), BF16),
            pltpu.VMEM((4, DEEP, HALF), BF16),
            pltpu.VMEM((4, PROBES, HALF), F32),
            pltpu.VMEM((8, PROBES, HALF), F32),
            pltpu.VMEM((PROBES, 128), F32),
            pltpu.VMEM((16, PROBES, 128), F32),
            pltpu.VMEM((8, PROBES, 128), F32),
            dma((4, 4)), dma((4, 4)), dma((4,)), dma((4, 2)), dma((1,)), dma((15,)), dma((7,)),
            dma((4, 4)), dma((4, 4)), dma((4,)), dma((8,)), dma((1,)), dma((16,)), dma((8,)),
        ],
        compiler_params=pltpu.CompilerParams(
            collective_id=0, has_side_effects=True, vmem_limit_bytes=56 << 20
        ),
        cost_estimate=pl.CostEstimate(flops=5_000_000_000, bytes_accessed=1_000_000, transcendentals=17_000_000),
        name="cg_step",
    )(descriptors, ard_scales.reshape(1, FEAT), noise.reshape(1, SHARD), probes)
    alpha, beta = scalars[:, 0:1], scalars[:, 1:2]
    residual = probes - alpha * image
    return alpha * probes, residual, residual + beta * probes


def solution(mesh):
    return jax.shard_map(
        local,
        mesh=mesh,
        in_specs=(P("loop", None), P(), P("loop"), P(None, "loop")),
        out_specs=(P(None, "loop"), P(None, "loop"), P(None, "loop")),
        check_vma=False,
    )
```

time: 485 us -> 56.3 us (0.12)
  blocking collectives: 312 us -> 0 us
  waiting for transfers between devices: 61.1 us -> 0 us
  matrix products: 54.7 us -> 0 us
  Pallas kernels: 0 us -> 52.9 us
  local copies, waits for them, and re-layouts: 35.1 us -> 0.96 us
  between operations: 14.1 us -> 0.65 us
    all_gather x1 -> x0, blocking collectives: 161 us -> none  [local(): piece_vector = lax.all_gather(source_vector, 'loop', axis=1, tiled=True)]
    psum x2 -> x0, blocking collectives: 151 us -> none  [the longest x1 77 us: cg_update(): norm_old = lax.psum(norm_local, ('loop', 'rep'))]
    psum x1 -> x0, waiting for transfers between devices: 61.1 us -> none  [local(): product = lax.psum(partial_sum, 'rep')]
    dot_general x32 -> x0, matrix products: 54.7 us -> none  [one_block(): jnp.dot(block_vector, kernel, preferred_element_type=jnp.float32)]
    pallas_call x0 -> x1, Pallas kernels: none -> 52.9 us  [local(): pl.pallas_call(kernel, out_shape=(jax.ShapeDtypeStruct((PROBES, SHARD), F...]
    dynamic_slice x64 -> x0, local copies, waits for them, and re-layouts: 33.1 us -> none  [one_block(): lax.dynamic_slice_in_dim(piece_scaled, block_index * width, width, 1)]
  transfers between devices with their start and end apart: 2 -> 0, of which waited for: 1 -> 0; matrix products, arithmetic and copies ran while one was open for 0% -> 0% of each run, Pallas kernels for 0% -> 0%
where the time goes in v1:
time: 56.3 us; the launch traced here: 56.1 us
  Pallas kernels  52.9 us (94%)
  other arithmetic  1.6 us (3%)
  local copies, waits for them, and re-layouts  0.96 us (2%)
  between operations  0.65 us (1%)
    pallas_call x1, Pallas kernels, local(): pl.pallas_call(kernel, out_shape=(jax.ShapeDtypeStruct((PROBES, SHARD), F...  52.9 us
    add x1, other arithmetic, local(): return (alpha * probes, residual, residual + beta * probes)  1.6 us

profile of v1, /device:TPU:1, one launch (start us, length us, event | category | flops | bytes accessed | tf_op | source)
XLA Modules:
  0.0 56.1 jit_solution(8920839683452962706)
XLA Ops:
  0.6 0.0 copy-start
  0.6 52.9 %cg_step.1 = (f32[16,1024]{1,0:T(8,128)}, f32[16,128]{1,0:T(8,128)}) custom-call(bf16[1024,128]{1,0:T(8,128)(2,1)} %desc_ref.1, f32[1,128]{1,0:T(1,128)} %bitcast.3, f32[1,1024]{1,0:T(1,128)} %bitcast.2, f32[16,1024]{1,0:T(8,128)} %probes_ref.1), custom_call_target="tpu_custom_call" | custom-call | flops 5000000000 | bytes 1000000 | tf_op jit(solution)/shard_map/cg_step/pallas_call | solution.py:305
  53.6 1.0 %slice_reduce_fusion = (f32[16]{0:T(128)S(1)}, f32[16]{0:T(128)S(1)}) fusion(f32[16,128]{1,0:T(8,128)} %get-tuple-element.5), kind=kLoop, calls=%fused_computation.3 | loop fusion | bytes 256 | tf_op jit(solution)/shard_map/slice | solution.py:330
  54.5 0.0 copy-done
  54.5 1.6 %multiply_add_fusion = (f32[16,1024]{1,0:T(8,128)}, f32[16,1024]{1,0:T(8,128)}, f32[16,1024]{1,0:T(8,128)}) fusion(f32[16,1024]{1,0:T(8,128)S(1)} %copy-done, f32[16]{0:T(128)S(1)} %get-tuple-element.7, f32[16,1024]{1,0:T(8,128)} %get-tuple-element.6, f32[16]{0:T(128)S(1)} %get-tuple-element.8), kind=kLoop, calls=%fused_computation | loop fusion | flops 81920 | bytes 327808 | tf_op jit(solution)/shard_map/add | solution.py:332
Async XLA Ops:
  0.6 53.9 %copy-start = (f32[16,1024]{1,0:T(8,128)S(1)}, f32[16,1024]{1,0:T(8,128)}, u32[]{:S(2)}) copy-start(f32[16,1024]{1,0:T(8,128)} %probes_ref.1) | copy-start | bytes 196612

commit v2 on v1

v2 whole, which is shorter than its diff:
```python
import functools

import jax
import jax.numpy as jnp
from jax import lax
from jax.experimental import pallas as pl
from jax.experimental.pallas import tpu as pltpu
from jax.sharding import PartitionSpec as P

MESH = pl.DeviceIdType.MESH
F32 = jnp.float32
BF16 = jnp.bfloat16

FEAT = 128
AUG = 16
PROBES = 16
SHARD = 1024
HALF = 512
QUART = 256
DEEP = FEAT + AUG
PACK = FEAT + AUG + PROBES

PAIRS = (
    ((0, 0), (0, 1)),
    ((-1, 0), (1, 0)),
    ((-2, 0), (2, 0)),
    ((-1, 1), (1, 1)),
    ((-3, 0), (3, 0)),
    ((-2, 1), (2, 1)),
    ((4, 0), (-3, 1)),
    ((3, 1), (4, 1)),
)
PLACE = {piece: (g, i) for g, pair in enumerate(PAIRS) for i, piece in enumerate(pair)}
UP = {(0, 0): (-1, 0), (-1, 0): (-2, 0), (-2, 0): (-3, 0), (-3, 0): (4, 0), (-2, 1): (-3, 1)}
DOWN = {(0, 0): (1, 0), (1, 0): (2, 0), (2, 0): (3, 0), (2, 1): (3, 1), (3, 1): (4, 1)}
ACROSS = {(0, 0): (0, 1), (-1, 0): (-1, 1), (1, 0): (1, 1), (-2, 0): (-2, 1), (2, 0): (2, 1)}
TARGET_X = (0, 1, 3, 2)
NEAR = (
    (0, 0, 0, 1, 0), (0, 0, 0, 7, 0), (0, 1, 1, 0, 0), (0, 0, 0, 0, 1), (0, 0, 1, 0, 0),
    (1, 0, 0, 0, 0), (3, 0, 0, 0, 0), (2, 0, 0, 0, 0),
)
PEERS = sorted(
    ((dx, dy, dz) for dx in range(4) for dy in range(2) for dz in range(8) if dx or dy or dz),
    key=lambda o: -(min(o[0], 4 - o[0]) + o[1] + min(o[2], 8 - o[2])),
)


def kernel(
    desc_hbm, ard_hbm, noise_hbm, probes_hbm, solution_ref, residual_ref, direction_ref,
    desc_s, desc_t, ard_ref, noise_ref, probes_ref, sbuf, tbuf, acc, reduced, image_ref, rows, sums,
    in_sem, ring_send, core_send, t_send, r_send, i_send, row_send, sum_send,
    ring_recv, core_recv, t_recv, r_recv, i_recv, row_recv, sum_recv,
):
    loop = lax.axis_index("loop")
    rep = lax.axis_index("rep")
    z, yh, x = loop // 8, (loop // 4) % 2, loop % 4
    yl, c = rep // 2, rep % 2

    def device(dx=0, dh=0, dl=0, dz=0, dc=0):
        nz = (z + dz) % 8
        nh = (yh + dh) % 2
        nx = (x + dx) % 4
        nl = (yl + dl) % 2
        nc = (c + dc) % 2
        return (nz * 8 + nh * 4 + nx, nl * 2 + nc)

    barrier = pltpu.get_barrier_semaphore()
    for offsets in NEAR:
        pl.semaphore_signal(barrier, inc=1, device_id=device(*offsets), device_id_type=MESH)

    half_at = pl.multiple_of(c * HALF, HALF)
    share = (yl + yh) % 2
    source_at = pl.multiple_of(share * HALF + c * QUART, QUART)

    fetches = [
        pltpu.make_async_copy(src, dst, in_sem.at[n])
        for n, (src, dst) in enumerate((
            (desc_hbm.at[pl.ds(source_at, QUART)], desc_s),
            (ard_hbm, ard_ref),
            (probes_hbm, probes_ref),
            (desc_hbm.at[pl.ds(half_at, HALF)], desc_t),
            (noise_hbm, noise_ref),
        ))
    ]
    for fetch in fetches:
        fetch.start()

    def prepare(points):
        values = points.astype(F32)
        mean = jnp.mean(values * values, axis=1, keepdims=True)
        unit = values * lax.rsqrt(mean + 1e-06)
        scaled = (unit * ard_ref[...]).astype(BF16)
        turned = scaled.astype(F32).T
        norm = -0.5 * jnp.sum(turned * turned, axis=0, keepdims=True)
        high = norm.astype(BF16).astype(F32)
        rest = norm - high
        mid = rest.astype(BF16).astype(F32)
        low = rest - mid
        return turned.astype(BF16), (high, mid, low)

    def extra(parts, first):
        count = parts[0].shape[1]
        row = lax.broadcasted_iota(jnp.int32, (AUG, count), 0)
        ones = 3 - first
        out = jnp.where((row >= ones) & (row < ones + 3), 1.0, 0.0)
        for n, part in enumerate(parts):
            out = jnp.where(row == first + n, part, out)
        return out.astype(BF16)

    def own(i):
        return pl.ds(pl.multiple_of(i * HALF + c * QUART, QUART), QUART)

    started = {}

    def begin(key, make):
        make().start()
        started[key] = make

    def copy(src, dst, send, recv, to):
        return pltpu.make_async_remote_copy(
            src_ref=src, dst_ref=dst, send_sem=send, recv_sem=recv, device_id=to, device_id_type=MESH
        )

    def ring(src, dst, to):
        (g, i), (h, j) = PLACE[src], PLACE[dst]
        return copy(
            sbuf.at[g, :, own(i)], sbuf.at[h, :, own(j)], ring_send.at[h, j], ring_recv.at[h, j], to
        )

    ways = ((UP, device(dz=1)), (DOWN, device(dz=7)), (ACROSS, device(dh=1, dl=1)))
    sibling = device(dc=1)

    def to_core(piece):
        g, i = PLACE[piece]
        return copy(
            sbuf.at[g, :, own(i)], sbuf.at[g, :, own(i)], core_send.at[g, i], core_recv.at[g, i], sibling
        )

    def from_core(pair):
        for i in range(2):
            there = pl.ds(pl.multiple_of(i * HALF + (1 - c) * QUART, QUART), QUART)
            copy(
                sbuf.at[pair, :, there], sbuf.at[pair, :, there], core_send.at[pair, i],
                core_recv.at[pair, i], sibling,
            ).wait_recv()

    def forward(piece):
        for table, to in ways:
            if piece in table:
                begin(("ring", table[piece]), functools.partial(ring, piece, table[piece], to))
        begin(("core", piece), functools.partial(to_core, piece))

    def arrive(*pieces):
        for piece in pieces:
            ring(piece, piece, ways[0][1]).wait_recv()
            forward(piece)

    def quarter(t):
        return tbuf.at[t // 2, :, pl.ds(t % 2 * HALF, HALF)]

    def target_copy(t):
        return copy(quarter(0), quarter(t), t_send.at[t], t_recv.at[t], device(dx=(4 - TARGET_X[t]) % 4))

    for n in (0, 1, 2):
        fetches[n].wait()
    turned, parts = prepare(desc_s[...])
    sbuf[0, 0:FEAT, own(0)] = turned
    sbuf[0, FEAT:DEEP, own(0)] = extra(parts, 0)
    sbuf[0, DEEP:PACK, own(0)] = probes_ref[:, pl.ds(source_at, QUART)].astype(BF16)
    pl.semaphore_wait(barrier, len(NEAR))
    forward((0, 0))
    fetches[3].wait()
    turned, parts = prepare(desc_t[...])
    tbuf[0, 0:FEAT, 0:HALF] = turned
    tbuf[0, FEAT:DEEP, 0:HALF] = extra(parts, 3)
    for t in (1, 2, 3):
        begin(("t", t), functools.partial(target_copy, t))
    fetches[4].wait()
    acc[...] = jnp.zeros_like(acc)

    def block(pairs, targets):
        whole = None
        for pair in pairs:
            cross = lax.dot_general(
                sbuf[pair, 0:DEEP, :], targets, (((0,), (0,)), ((), ())), preferred_element_type=F32
            )
            weights = jnp.exp(jnp.minimum(cross, 0.0)).astype(BF16)
            part = jnp.dot(sbuf[pair, DEEP:PACK, :], weights, preferred_element_type=F32)
            whole = part if whole is None else whole + part
        return whole

    def quarter_of(t):
        return tbuf[t // 2, :, pl.ds(pl.multiple_of(t % 2 * HALF, HALF), HALF)]

    def events(step, table):
        for at, action in table.items():
            pl.when(step == at)(action)

    arrive((-1, 0), (1, 0), (0, 1))
    from_core(0)
    from_core(1)

    def target_here(t):
        return lambda: target_copy(t).wait_recv()

    def last_target():
        arrive((-2, 0), (2, 0))
        target_copy(3).wait_recv()

    def first(t, carry):
        events(t, {1: target_here(1), 2: target_here(2), 3: last_target})
        acc[t] += block((0, 1), quarter_of(t))
        return carry

    lax.fori_loop(0, 4, first, 0)

    def at0():
        arrive((-1, 1), (1, 1))
        from_core(2)

    def at2():
        arrive((3, 0), (-3, 0))
        from_core(3)

    def at4():
        arrive((-2, 1))
        from_core(4)

    def at6():
        arrive((3, 1))
        from_core(5)

    def middle(n, carry):
        events(n, {
            0: at0,
            2: at2,
            3: lambda: arrive((2, 1)),
            4: at4,
            6: at6,
            7: lambda: arrive((4, 0), (-3, 1)),
            8: lambda: from_core(6),
            9: lambda: arrive((4, 1)),
        })
        h = n % 2
        part = block((2 + n // 2,), tbuf[h])
        acc[2 * h] += part[:, 0:HALF]
        acc[2 * h + 1] += part[:, HALF:]
        return carry

    lax.fori_loop(0, 10, middle, 0)
    from_core(7)

    mine = x * 2 + yl

    def reduce_copy(t, dl):
        return copy(
            acc.at[t], reduced.at[mine], r_send.at[t, dl], r_recv.at[mine], device(dx=TARGET_X[t], dl=dl)
        )

    def leave(t):
        def action():
            for dl in (1, 0) if t else (1,):
                begin(("r", t, dl), functools.partial(reduce_copy, t, dl))
        return action

    def last(n, carry):
        t = 3 - n
        acc[t] += block((7,), quarter_of(t))
        events(t, {s: leave(s) for s in (3, 2, 1, 0)})
        return carry

    lax.fori_loop(0, 4, last, 0)
    reduced[mine] = acc[0]
    rhs = probes_ref[:, pl.ds(half_at, HALF)]
    diagonal = noise_ref[:, pl.ds(half_at, HALF)] * rhs
    norm = jnp.sum(rhs * rhs, axis=1, keepdims=True)
    for t in (3, 2, 1, 0):
        for dl in (1, 0) if t else (1,):
            other = ((x + TARGET_X[t]) % 4) * 2 + (yl + dl) % 2
            copy(
                acc.at[t], reduced.at[other], r_send.at[t, dl], r_recv.at[other], device(dx=TARGET_X[t], dl=dl)
            ).wait_recv()

    total = reduced[0]
    for n in range(1, 8):
        total = total + reduced[n]
    image = total + diagonal
    curve = jnp.sum(rhs * image, axis=1, keepdims=True)
    square = jnp.sum(image * image, axis=1, keepdims=True)

    lane = lax.broadcasted_iota(jnp.int32, (PROBES, 128), 1)
    probe = lax.broadcasted_iota(jnp.int32, (PROBES, 128), 0)
    spread = jnp.zeros((PROBES, 128), F32)
    for n, column in enumerate((norm, curve, square)):
        spread = jnp.where(lane == probe + PROBES * n, column, spread)
    rows[pl.ds(c, 1), :] = jnp.sum(spread, axis=0, keepdims=True)

    def row_copy(at):
        return copy(rows.at[pl.ds(at, 1)], rows.at[pl.ds(at, 1)], row_send.at[0], row_recv.at[0], sibling)

    begin("row", functools.partial(row_copy, c))
    span = pl.ds(half_at, HALF)
    image_ref[:, span] = image

    def image_copy(at):
        return copy(image_ref.at[:, at], image_ref.at[:, at], i_send.at[0], i_recv.at[0], sibling)

    row_copy(1 - c).wait_recv()
    sums[pl.ds(loop, 1), :] = rows[0:1, :] + rows[1:2, :]
    for dx, dy, dz in PEERS:
        copy(
            sums.at[pl.ds(loop, 1)], sums.at[pl.ds(loop, 1)], sum_send.at[0], sum_recv.at[0],
            device(dx=dx, dh=dy, dl=dy, dz=dz),
        ).start()
    begin("image", functools.partial(image_copy, span))
    image_copy(pl.ds(pl.multiple_of((1 - c) * HALF, HALF), HALF)).wait_recv()
    for make in started.values():
        make().wait_send()

    others = copy(
        sums.at[pl.ds(0, len(PEERS))], sums.at[pl.ds(0, len(PEERS))], sum_send.at[0], sum_recv.at[0], sibling
    )
    others.wait_recv()
    summed = jnp.sum(sums[...], axis=0, keepdims=True)

    def column(n):
        return jnp.sum(jnp.where(lane == probe + PROBES * n, summed, 0.0), axis=1, keepdims=True)

    norm, curve, square = column(0), column(1), column(2)
    alpha = norm / curve
    beta = jnp.maximum(alpha * alpha * square - norm, 0.0) / norm
    rhs = probes_ref[...]
    residual = rhs - alpha * image_ref[...]
    solution_ref[...] = alpha * rhs
    residual_ref[...] = residual
    direction_ref[...] = residual + beta * rhs
    others.wait_send()


def local(descriptors, ard_scales, noise, probes):
    dma = pltpu.SemaphoreType.DMA
    shape = jax.ShapeDtypeStruct((PROBES, SHARD), F32)
    return pl.pallas_call(
        kernel,
        out_shape=(shape, shape, shape),
        in_specs=[pl.BlockSpec(memory_space=pl.ANY)] * 4,
        out_specs=(pl.BlockSpec(memory_space=pltpu.VMEM),) * 3,
        scratch_shapes=[
            pltpu.VMEM((QUART, FEAT), BF16),
            pltpu.VMEM((HALF, FEAT), BF16),
            pltpu.VMEM((1, FEAT), F32),
            pltpu.VMEM((1, SHARD), F32),
            pltpu.VMEM((PROBES, SHARD), F32),
            pltpu.VMEM((8, PACK, 2 * HALF), BF16),
            pltpu.VMEM((2, DEEP, 2 * HALF), BF16),
            pltpu.VMEM((4, PROBES, HALF), F32),
            pltpu.VMEM((8, PROBES, HALF), F32),
            pltpu.VMEM((PROBES, SHARD), F32),
            pltpu.VMEM((8, 128), F32),
            pltpu.VMEM((64, 128), F32),
            dma((5,)),
            dma((8, 2)), dma((8, 2)), dma((4,)), dma((4, 2)), dma((1,)), dma((1,)), dma((1,)),
            dma((8, 2)), dma((8, 2)), dma((4,)), dma((8,)), dma((1,)), dma((1,)), dma((1,)),
        ],
        compiler_params=pltpu.CompilerParams(
            collective_id=0, has_side_effects=True, vmem_limit_bytes=56 << 20
        ),
        cost_estimate=pl.CostEstimate(flops=5_000_000_000, bytes_accessed=1_000_000, transcendentals=17_000_000),
        name="cg_step",
    )(descriptors, ard_scales.reshape(1, FEAT), noise.reshape(1, SHARD), probes)


def solution(mesh):
    return jax.shard_map(
        local,
        mesh=mesh,
        in_specs=(P("loop", None), P(), P("loop"), P(None, "loop")),
        out_specs=(P(None, "loop"), P(None, "loop"), P(None, "loop")),
        check_vma=False,
    )
```

time: 56.3 us -> 51.1 us (0.908)
  Pallas kernels: 52.9 us -> 47.3 us
  local copies, waits for them, and re-layouts: 0.96 us -> 3 us
  other arithmetic: 1.6 us -> 0 us
    pallas_call x1, Pallas kernels: 52.9 us -> 47.3 us  [local(): pl.pallas_call(kernel, out_shape=(shape, shape, shape), in_specs=[pl.Bloc...]
    unnamed x2 -> x7, local copies, waits for them, and re-layouts: 0.01 us -> 3 us
    add x1 -> x0, other arithmetic: 1.6 us -> none  [local(): return (alpha * probes, residual, residual + beta * probes)]
    slice x1 -> x0, local copies, waits for them, and re-layouts: 0.95 us -> none  [local(): alpha, beta = (scalars[:, 0:1], scalars[:, 1:2])]
where the time goes in v2:
time: 51.1 us; the launch traced here: 51 us
  Pallas kernels  47.3 us (93%)
  local copies, waits for them, and re-layouts  3 us (6%)
  between operations  0.65 us (1%)
    pallas_call x1, Pallas kernels, local(): pl.pallas_call(kernel, out_shape=(shape, shape, shape), in_specs=[pl.Bloc...  47.3 us
    unnamed x7, local copies, waits for them, and re-layouts  3 us

profile of v2, /device:TPU:1, one launch (start us, length us, event | category | flops | bytes accessed | tf_op | source)
XLA Modules:
  0.0 51.0 jit_solution(4419595900155922720)
XLA Ops:
  0.6 47.3 %cg_step.1 = (f32[16,1024]{1,0:T(8,128)}, f32[16,1024]{1,0:T(8,128)}, f32[16,1024]{1,0:T(8,128)}) custom-call(bf16[1024,128]{1,0:T(8,128)(2,1)} %desc_hbm.1, f32[1,128]{1,0:T(1,128)} %bitcast.3, f32[1,1024]{1,0:T(1,128)} %bitcast.2, f32[16,1024]{1,0:T(8,128)} %probes_hbm.1), custom_call_target="tpu_custom_call" | custom-call | flops 5000000000 | bytes 1000000 | tf_op jit(solution)/shard_map/cg_step/pallas_call | solution.py:343
  47.9 0.0 copy-start.1
  48.0 1.5 %copy.10 = f32[16,1024]{1,0:T(8,128)} copy(f32[16,1024]{1,0:T(8,128)} %get-tuple-element.6) | data formatting | bytes 131072
  49.5 0.0 copy-done.1
  49.5 0.0 copy-start
  49.5 0.6 %copy.11 = f32[16,1024]{1,0:T(8,128)} copy(f32[16,1024]{1,0:T(8,128)S(1)} %copy-done.1) | data formatting | bytes 131072
  50.1 0.2 copy-done
  50.3 0.6 %copy.12 = f32[16,1024]{1,0:T(8,128)} copy(f32[16,1024]{1,0:T(8,128)S(1)} %copy-done) | data formatting | bytes 131072
Async XLA Ops:
  47.9 1.5 %copy-start.1 = (f32[16,1024]{1,0:T(8,128)S(1)}, f32[16,1024]{1,0:T(8,128)}, u32[]{:S(2)}) copy-start(f32[16,1024]{1,0:T(8,128)} %get-tuple-element.7) | copy-start | bytes 196612
  49.5 0.9 %copy-start = (f32[16,1024]{1,0:T(8,128)S(1)}, f32[16,1024]{1,0:T(8,128)}, u32[]{:S(2)}) copy-start(f32[16,1024]{1,0:T(8,128)} %get-tuple-element.8) | copy-start | bytes 196612

commit v3 on v2

--- a/solution.py
+++ b/solution.py
@@ -19,6 +19,7 @@
 QUART = 256
 DEEP = FEAT + AUG
 PACK = FEAT + AUG + PROBES
+PART = 128
 
 PAIRS = (
     ((0, 0), (0, 1)),
@@ -27,9 +28,10 @@
     ((-1, 1), (1, 1)),
     ((-3, 0), (3, 0)),
     ((-2, 1), (2, 1)),
-    ((4, 0), (-3, 1)),
-    ((3, 1), (4, 1)),
+    ((4, 0), (3, 1)),
+    ((-3, 1), (4, 1)),
 )
+SPLIT = 4
 PLACE = {piece: (g, i) for g, pair in enumerate(PAIRS) for i, piece in enumerate(pair)}
 UP = {(0, 0): (-1, 0), (-1, 0): (-2, 0), (-2, 0): (-3, 0), (-3, 0): (4, 0), (-2, 1): (-3, 1)}
 DOWN = {(0, 0): (1, 0), (1, 0): (2, 0), (2, 0): (3, 0), (2, 1): (3, 1), (3, 1): (4, 1)}
@@ -46,8 +48,8 @@
 
 
 def kernel(
-    desc_hbm, ard_hbm, noise_hbm, probes_hbm, solution_ref, residual_ref, direction_ref,
-    desc_s, desc_t, ard_ref, noise_ref, probes_ref, sbuf, tbuf, acc, reduced, image_ref, rows, sums,
+    desc_hbm, ard_hbm, noise_hbm, probes_hbm, alpha_ref, image_ref, beta_ref,
+    desc_s, desc_t, ard_ref, noise_ref, probes_ref, sbuf, tbuf, acc, parting, reduced, rows, sums,
     in_sem, ring_send, core_send, t_send, r_send, i_send, row_send, sum_send,
     ring_recv, core_recv, t_recv, r_recv, i_recv, row_recv, sum_recv,
 ):
@@ -107,8 +109,13 @@
             out = jnp.where(row == first + n, part, out)
         return out.astype(BF16)
 
-    def own(i):
-        return pl.ds(pl.multiple_of(i * HALF + c * QUART, QUART), QUART)
+    def place(piece, core, part):
+        g, i = PLACE[piece]
+        points = pl.ds(pl.multiple_of(i * QUART + core * PART, PART), PART)
+        return sbuf.at[g, :, :, points] if part is None else sbuf.at[g, part, :, points]
+
+    def parts_of(piece):
+        return (0, 1) if PLACE[piece][0] < SPLIT else (None,)
 
     started = {}
 
@@ -121,73 +128,88 @@
             src_ref=src, dst_ref=dst, send_sem=send, recv_sem=recv, device_id=to, device_id_type=MESH
         )
 
-    def ring(src, dst, to):
-        (g, i), (h, j) = PLACE[src], PLACE[dst]
-        return copy(
-            sbuf.at[g, :, own(i)], sbuf.at[h, :, own(j)], ring_send.at[h, j], ring_recv.at[h, j], to
-        )
+    def ring(src, dst, part, to):
+        at = PLACE[dst] + (part or 0,)
+        return copy(place(src, c, part), place(dst, c, part), ring_send.at[at], ring_recv.at[at], to)
 
     ways = ((UP, device(dz=1)), (DOWN, device(dz=7)), (ACROSS, device(dh=1, dl=1)))
     sibling = device(dc=1)
 
-    def to_core(piece):
-        g, i = PLACE[piece]
-        return copy(
-            sbuf.at[g, :, own(i)], sbuf.at[g, :, own(i)], core_send.at[g, i], core_recv.at[g, i], sibling
-        )
-
-    def from_core(pair):
-        for i in range(2):
-            there = pl.ds(pl.multiple_of(i * HALF + (1 - c) * QUART, QUART), QUART)
-            copy(
-                sbuf.at[pair, :, there], sbuf.at[pair, :, there], core_send.at[pair, i],
-                core_recv.at[pair, i], sibling,
-            ).wait_recv()
-
-    def forward(piece):
+    def core_copy(piece, part, core):
+        at = PLACE[piece] + (part or 0,)
+        return copy(place(piece, core, part), place(piece, core, part), core_send.at[at], core_recv.at[at], sibling)
+
+    def from_core(pair, part=None):
+        for piece in PAIRS[pair]:
+            for p in parts_of(piece):
+                if part is None or p == part:
+                    core_copy(piece, p, 1 - c).wait_recv()
+
+    def forward(piece, part):
         for table, to in ways:
             if piece in table:
-                begin(("ring", table[piece]), functools.partial(ring, piece, table[piece], to))
-        begin(("core", piece), functools.partial(to_core, piece))
-
-    def arrive(*pieces):
-        for piece in pieces:
-            ring(piece, piece, ways[0][1]).wait_recv()
-            forward(piece)
-
-    def quarter(t):
-        return tbuf.at[t // 2, :, pl.ds(t % 2 * HALF, HALF)]
+                onward = table[piece]
+                for p in parts_of(onward) if part is None else (part,):
+                    begin(("ring", onward, p), functools.partial(ring, piece, onward, p, to))
+        begin(("core", piece, part), functools.partial(core_copy, piece, part, c))
+
+    def arrive(piece, part=None):
+        for p in parts_of(piece) if part is None else (part,):
+            ring(piece, piece, p, ways[0][1]).wait_recv()
+        if part is None and parts_of(piece) == (0, 1):
+            for table, to in ways:
+                if piece in table:
+                    begin(("ring", table[piece], None), functools.partial(ring, piece, table[piece], None, to))
+            for p in (0, 1):
+                begin(("core", piece, p), functools.partial(core_copy, piece, p, c))
+        else:
+            forward(piece, part)
+
+    def target(t, first=0, count=HALF):
+        return tbuf.at[t // 2, :, pl.ds(t % 2 * HALF + first, count)]
 
     def target_copy(t):
-        return copy(quarter(0), quarter(t), t_send.at[t], t_recv.at[t], device(dx=(4 - TARGET_X[t]) % 4))
+        return copy(target(0), target(t), t_send.at[t], t_recv.at[t], device(dx=(4 - TARGET_X[t]) % 4))
+
+    def target_relay(t):
+        half = (t - 1) * QUART
+        return copy(
+            target(t, half, QUART), target(3, half, QUART), t_send.at[t + 2], t_recv.at[t + 2],
+            device(dx=(4 - TARGET_X[t]) % 4),
+        )
 
     for n in (0, 1, 2):
         fetches[n].wait()
     turned, parts = prepare(desc_s[...])
-    sbuf[0, 0:FEAT, own(0)] = turned
-    sbuf[0, FEAT:DEEP, own(0)] = extra(parts, 0)
-    sbuf[0, DEEP:PACK, own(0)] = probes_ref[:, pl.ds(source_at, QUART)].astype(BF16)
-    pl.semaphore_wait(barrier, len(NEAR))
-    forward((0, 0))
+    norms = extra(parts, 0)
+    vector = probes_ref[:, pl.ds(source_at, QUART)].astype(BF16)
+    points = pl.ds(pl.multiple_of(c * PART, PART), PART)
+    for part in (0, 1):
+        span = slice(part * PART, (part + 1) * PART)
+        sbuf[0, part, 0:FEAT, points] = turned[:, span]
+        sbuf[0, part, FEAT:DEEP, points] = norms[:, span]
+        sbuf[0, part, DEEP:PACK, points] = vector[:, span]
     fetches[3].wait()
     turned, parts = prepare(desc_t[...])
     tbuf[0, 0:FEAT, 0:HALF] = turned
     tbuf[0, FEAT:DEEP, 0:HALF] = extra(parts, 3)
-    for t in (1, 2, 3):
+    pl.semaphore_wait(barrier, len(NEAR))
+    forward((0, 0), 0)
+    for t in (1, 2):
         begin(("t", t), functools.partial(target_copy, t))
+    forward((0, 0), 1)
     fetches[4].wait()
     acc[...] = jnp.zeros_like(acc)
 
-    def block(pairs, targets):
-        whole = None
-        for pair in pairs:
-            cross = lax.dot_general(
-                sbuf[pair, 0:DEEP, :], targets, (((0,), (0,)), ((), ())), preferred_element_type=F32
-            )
-            weights = jnp.exp(jnp.minimum(cross, 0.0)).astype(BF16)
-            part = jnp.dot(sbuf[pair, DEEP:PACK, :], weights, preferred_element_type=F32)
-            whole = part if whole is None else whole + part
-        return whole
+    def block(sources, targets):
+        cross = lax.dot_general(
+            sources[0:DEEP], targets, (((0,), (0,)), ((), ())), preferred_element_type=F32
+        )
+        weights = jnp.exp(jnp.minimum(cross, 0.0)).astype(BF16)
+        return jnp.dot(sources[DEEP:PACK], weights, preferred_element_type=F32)
+
+    def pair_of(g):
+        return jnp.concatenate([sbuf[g, 0], sbuf[g, 1]], axis=1)
 
     def quarter_of(t):
         return tbuf[t // 2, :, pl.ds(pl.multiple_of(t % 2 * HALF, HALF), HALF)]
@@ -196,30 +218,54 @@
         for at, action in table.items():
             pl.when(step == at)(action)
 
-    arrive((-1, 0), (1, 0), (0, 1))
-    from_core(0)
-    from_core(1)
+    def part_here(part):
+        def action():
+            for piece in ((-1, 0), (1, 0), (0, 1)):
+                arrive(piece, part)
+            from_core(0, part)
+            from_core(1, part)
+        return action
+
+    def begins(part, carry):
+        events(part, {0: part_here(0), 1: part_here(1)})
+        acc[0] += block(jnp.concatenate([sbuf[0, part], sbuf[1, part]], axis=1), tbuf[0, :, 0:HALF])
+        return carry
+
+    lax.fori_loop(0, 2, begins, 0)
 
     def target_here(t):
-        return lambda: target_copy(t).wait_recv()
-
-    def last_target():
-        arrive((-2, 0), (2, 0))
-        target_copy(3).wait_recv()
-
-    def first(t, carry):
-        events(t, {1: target_here(1), 2: target_here(2), 3: last_target})
-        acc[t] += block((0, 1), quarter_of(t))
+        def action():
+            target_copy(t).wait_recv()
+            begin(("t", t + 2), functools.partial(target_relay, t))
+        return action
+
+    def second():
+        for piece in ((-2, 0), (2, 0)):
+            arrive(piece)
+
+    def first(m, carry):
+        events(m, {0: target_here(1), 2: target_here(2), 3: second})
+        t = 1 + m // 2
+        acc[t] += block(pair_of(m % 2), quarter_of(t))
         return carry
 
     lax.fori_loop(0, 4, first, 0)
 
     def at0():
-        arrive((-1, 1), (1, 1))
         from_core(2)
 
+    def at1():
+        arrive((-1, 1))
+        arrive((1, 1))
+        for t in (1, 2):
+            target_relay(t).wait_recv()
+        for g in (0, 1):
+            acc[3] += block(pair_of(g), tbuf[1, :, HALF:])
+
     def at2():
-        arrive((3, 0), (-3, 0))
+        arrive((3, 0))
+        arrive((-3, 0))
+        arrive((2, 1))
         from_core(3)
 
     def at4():
@@ -230,19 +276,23 @@
         arrive((3, 1))
         from_core(5)
 
+    def at9():
+        arrive((-3, 1))
+        arrive((4, 1))
+
     def middle(n, carry):
         events(n, {
             0: at0,
+            1: at1,
             2: at2,
-            3: lambda: arrive((2, 1)),
             4: at4,
             6: at6,
-            7: lambda: arrive((4, 0), (-3, 1)),
+            7: lambda: arrive((4, 0)),
             8: lambda: from_core(6),
-            9: lambda: arrive((4, 1)),
+            9: at9,
         })
         h = n % 2
-        part = block((2 + n // 2,), tbuf[h])
+        part = block(pair_of(2 + n // 2), tbuf[h])
         acc[2 * h] += part[:, 0:HALF]
         acc[2 * h + 1] += part[:, HALF:]
         return carry
@@ -254,7 +304,7 @@
 
     def reduce_copy(t, dl):
         return copy(
-            acc.at[t], reduced.at[mine], r_send.at[t, dl], r_recv.at[mine], device(dx=TARGET_X[t], dl=dl)
+            parting.at[t], reduced.at[mine], r_send.at[t, dl], r_recv.at[mine], device(dx=TARGET_X[t], dl=dl)
         )
 
     def leave(t):
@@ -265,12 +315,12 @@
 
     def last(n, carry):
         t = 3 - n
-        acc[t] += block((7,), quarter_of(t))
+        parting[t] = (acc[t] + block(pair_of(7), quarter_of(t))).astype(BF16)
         events(t, {s: leave(s) for s in (3, 2, 1, 0)})
         return carry
 
     lax.fori_loop(0, 4, last, 0)
-    reduced[mine] = acc[0]
+    reduced[mine] = parting[0]
     rhs = probes_ref[:, pl.ds(half_at, HALF)]
     diagonal = noise_ref[:, pl.ds(half_at, HALF)] * rhs
     norm = jnp.sum(rhs * rhs, axis=1, keepdims=True)
@@ -278,12 +328,12 @@
         for dl in (1, 0) if t else (1,):
             other = ((x + TARGET_X[t]) % 4) * 2 + (yl + dl) % 2
             copy(
-                acc.at[t], reduced.at[other], r_send.at[t, dl], r_recv.at[other], device(dx=TARGET_X[t], dl=dl)
+                parting.at[t], reduced.at[other], r_send.at[t, dl], r_recv.at[other], device(dx=TARGET_X[t], dl=dl)
             ).wait_recv()
 
-    total = reduced[0]
+    total = reduced[0].astype(F32)
     for n in range(1, 8):
-        total = total + reduced[n]
+        total = total + reduced[n].astype(F32)
     image = total + diagonal
     curve = jnp.sum(rhs * image, axis=1, keepdims=True)
     square = jnp.sum(image * image, axis=1, keepdims=True)
@@ -329,18 +379,15 @@
     norm, curve, square = column(0), column(1), column(2)
     alpha = norm / curve
     beta = jnp.maximum(alpha * alpha * square - norm, 0.0) / norm
-    rhs = probes_ref[...]
-    residual = rhs - alpha * image_ref[...]
-    solution_ref[...] = alpha * rhs
-    residual_ref[...] = residual
-    direction_ref[...] = residual + beta * rhs
+    alpha_ref[...] = jnp.broadcast_to(alpha, (PROBES, SHARD))
+    beta_ref[...] = jnp.broadcast_to(beta, (PROBES, SHARD))
     others.wait_send()
 
 
 def local(descriptors, ard_scales, noise, probes):
     dma = pltpu.SemaphoreType.DMA
-    shape = jax.ShapeDtypeStruct((PROBES, SHARD), F32)
-    return pl.pallas_call(
+    shape = pltpu.VMEM((PROBES, SHARD), F32)
+    alpha, image, beta = pl.pallas_call(
         kernel,
         out_shape=(shape, shape, shape),
         in_specs=[pl.BlockSpec(memory_space=pl.ANY)] * 4,
@@ -351,16 +398,16 @@
             pltpu.VMEM((1, FEAT), F32),
             pltpu.VMEM((1, SHARD), F32),
             pltpu.VMEM((PROBES, SHARD), F32),
-            pltpu.VMEM((8, PACK, 2 * HALF), BF16),
+            pltpu.VMEM((8, 2, PACK, HALF), BF16),
             pltpu.VMEM((2, DEEP, 2 * HALF), BF16),
             pltpu.VMEM((4, PROBES, HALF), F32),
-            pltpu.VMEM((8, PROBES, HALF), F32),
-            pltpu.VMEM((PROBES, SHARD), F32),
+            pltpu.VMEM((4, PROBES, HALF), BF16),
+            pltpu.VMEM((8, PROBES, HALF), BF16),
             pltpu.VMEM((8, 128), F32),
             pltpu.VMEM((64, 128), F32),
             dma((5,)),
-            dma((8, 2)), dma((8, 2)), dma((4,)), dma((4, 2)), dma((1,)), dma((1,)), dma((1,)),
-            dma((8, 2)), dma((8, 2)), dma((4,)), dma((8,)), dma((1,)), dma((1,)), dma((1,)),
+            dma((8, 2, 2)), dma((8, 2, 2)), dma((5,)), dma((4, 2)), dma((1,)), dma((1,)), dma((1,)),
+            dma((8, 2, 2)), dma((8, 2, 2)), dma((5,)), dma((8,)), dma((1,)), dma((1,)), dma((1,)),
         ],
         compiler_params=pltpu.CompilerParams(
             collective_id=0, has_side_effects=True, vmem_limit_bytes=56 << 20
@@ -368,6 +415,8 @@
         cost_estimate=pl.CostEstimate(flops=5_000_000_000, bytes_accessed=1_000_000, transcendentals=17_000_000),
         name="cg_step",
     )(descriptors, ard_scales.reshape(1, FEAT), noise.reshape(1, SHARD), probes)
+    residual = probes - alpha * image
+    return alpha * probes, residual, residual + beta * probes
 
 
 def solution(mesh):

time: 51.1 us -> 47.9 us (0.937)
  local copies, waits for them, and re-layouts: 3 us -> 0.01 us
  Pallas kernels: 47.3 us -> 46.5 us
  other arithmetic: 0 us -> 0.69 us
    unnamed x7 -> x2, local copies, waits for them, and re-layouts: 3 us -> 0.01 us
    pallas_call x1, Pallas kernels: 47.3 us -> 46.5 us  [local(): pl.pallas_call(kernel, out_shape=(shape, shape, shape), in_specs=[pl.Bloc...]
    add x0 -> x1, other arithmetic: none -> 0.69 us  [local(): return (alpha * probes, residual, residual + beta * probes)]
where the time goes in v3:
time: 47.9 us; the launch traced here: 47.8 us
  Pallas kernels  46.5 us (97%)
  other arithmetic  0.69 us (1%)
  between operations  0.65 us (1%)
    pallas_call x1, Pallas kernels, local(): pl.pallas_call(kernel, out_shape=(shape, shape, shape), in_specs=[pl.Bloc...  46.5 us

profile of v3, /device:TPU:1, one launch (start us, length us, event | category | flops | bytes accessed | tf_op | source)
XLA Modules:
  0.0 47.8 jit_solution(5425029819177861013)
XLA Ops:
  0.6 0.0 copy-start
  0.6 46.5 %cg_step.1 = (f32[16,1024]{1,0:T(8,128)S(1)}, f32[16,1024]{1,0:T(8,128)S(1)}, f32[16,1024]{1,0:T(8,128)S(1)}) custom-call(bf16[1024,128]{1,0:T(8,128)(2,1)} %desc_hbm.1, f32[1,128]{1,0:T(1,128)} %bitcast.3, f32[1,1024]{1,0:T(1,128)} %bitcast.2, f32[16,1024]{1,0:T(8,128)} %probes_hbm.1), custom_call_target="tpu_custom_call" | custom-call | flops 5000000000 | bytes 1000000 | tf_op jit(solution)/shard_map/cg_step/pallas_call | solution.py:390
  47.1 0.0 copy-done
  47.1 0.7 %multiply_add_fusion = (f32[16,1024]{1,0:T(8,128)}, f32[16,1024]{1,0:T(8,128)}, f32[16,1024]{1,0:T(8,128)}) fusion(f32[16,1024]{1,0:T(8,128)S(1)} %get-tuple-element.8, f32[16,1024]{1,0:T(8,128)S(1)} %copy-done, f32[16,1024]{1,0:T(8,128)S(1)} %get-tuple-element.6, f32[16,1024]{1,0:T(8,128)S(1)} %get-tuple-element.7), kind=kLoop, calls=%fused_computation | loop fusion | flops 81920 | bytes 458752 | tf_op jit(solution)/shard_map/add | solution.py:419
Async XLA Ops:
  0.6 46.5 %copy-start = (f32[16,1024]{1,0:T(8,128)S(1)}, f32[16,1024]{1,0:T(8,128)}, u32[]{:S(2)}) copy-start(f32[16,1024]{1,0:T(8,128)} %probes_hbm.1) | copy-start | bytes 196612

commit v4 on v3

--- a/solution.py
+++ b/solution.py
@@ -27,31 +27,36 @@
     ((-2, 0), (2, 0)),
     ((-1, 1), (1, 1)),
     ((-3, 0), (3, 0)),
-    ((-2, 1), (2, 1)),
-    ((4, 0), (3, 1)),
-    ((-3, 1), (4, 1)),
+    ((2, 1), (4, 0)),
+    ((-2, 1), (3, 1)),
+    ((4, 1), (-3, 1)),
 )
 SPLIT = 4
 PLACE = {piece: (g, i) for g, pair in enumerate(PAIRS) for i, piece in enumerate(pair)}
-UP = {(0, 0): (-1, 0), (-1, 0): (-2, 0), (-2, 0): (-3, 0), (-3, 0): (4, 0), (-2, 1): (-3, 1)}
-DOWN = {(0, 0): (1, 0), (1, 0): (2, 0), (2, 0): (3, 0), (2, 1): (3, 1), (3, 1): (4, 1)}
-ACROSS = {(0, 0): (0, 1), (-1, 0): (-1, 1), (1, 0): (1, 1), (-2, 0): (-2, 1), (2, 0): (2, 1)}
+UP = {(0, 0): (-1, 0), (-1, 0): (-2, 0), (-2, 0): (-3, 0), (-2, 1): (-3, 1)}
+DOWN = {(0, 0): (1, 0), (1, 0): (2, 0), (2, 0): (3, 0), (2, 1): (3, 1)}
+ACROSS = {(0, 0): (0, 1), (-1, 0): (-1, 1), (1, 0): (1, 1), (-2, 0): (-2, 1), (2, 0): (2, 1), (4, 0): (4, 1)}
+NEXT = ((-1, 0), (1, 0), (0, 1))
+ARRIVE = {0: ((((-1, 0), (1, 0), (0, 1)), 0),), 1: ((((-1, 0), (1, 0), (0, 1)), 1),), 6: ((((-2, 0), (2, 0)), None),), 7: ((((-1, 1), (1, 1)), None),), 8: ((((2, 1), (4, 0)), None),), 9: ((((3, 0), (-3, 0)), None),), 10: ((((-2, 1),), None),), 13: ((((3, 1),), None),), 14: ((((4, 1),), None),), 15: ((((-3, 1),), None),)}
+CORE = {0: ((0, 0), (1, 0)), 1: ((0, 1), (1, 1)), 6: ((2, None),), 8: ((3, None),), 10: ((4, None),), 12: ((5, None),), 14: ((6, None),), 16: ((7, None),)}
+TARGET = {2: (1,), 4: (2,)}
+FAR = 2
 TARGET_X = (0, 1, 3, 2)
 NEAR = (
     (0, 0, 0, 1, 0), (0, 0, 0, 7, 0), (0, 1, 1, 0, 0), (0, 0, 0, 0, 1), (0, 0, 1, 0, 0),
     (1, 0, 0, 0, 0), (3, 0, 0, 0, 0), (2, 0, 0, 0, 0),
 )
 PEERS = sorted(
-    ((dx, dy, dz) for dx in range(4) for dy in range(2) for dz in range(8) if dx or dy or dz),
+    ((dx, dy, dz, dc) for dx in range(4) for dy in range(2) for dz in range(8) for dc in range(2) if dx or dy or dz or dc),
     key=lambda o: -(min(o[0], 4 - o[0]) + o[1] + min(o[2], 8 - o[2])),
 )
 
 
 def kernel(
     desc_hbm, ard_hbm, noise_hbm, probes_hbm, alpha_ref, image_ref, beta_ref,
-    desc_s, desc_t, ard_ref, noise_ref, probes_ref, sbuf, tbuf, acc, parting, reduced, rows, sums,
-    in_sem, ring_send, core_send, t_send, r_send, i_send, row_send, sum_send,
-    ring_recv, core_recv, t_recv, r_recv, i_recv, row_recv, sum_recv,
+    desc_s, desc_t, ard_ref, noise_ref, probes_ref, sbuf, tbuf, acc, parting, reduced, sums,
+    in_sem, ring_send, core_send, t_send, r_send, i_send, sum_send,
+    ring_recv, core_recv, t_recv, r_recv, i_recv, sum_recv, ready1, ready2,
 ):
     loop = lax.axis_index("loop")
     rep = lax.axis_index("rep")
@@ -133,7 +138,7 @@
         return copy(place(src, c, part), place(dst, c, part), ring_send.at[at], ring_recv.at[at], to)
 
     ways = ((UP, device(dz=1)), (DOWN, device(dz=7)), (ACROSS, device(dh=1, dl=1)))
-    sibling = device(dc=1)
+    sibling, opposite = device(dc=1), device(dz=4)
 
     def core_copy(piece, part, core):
         at = PLACE[piece] + (part or 0,)
@@ -194,12 +199,17 @@
     tbuf[0, 0:FEAT, 0:HALF] = turned
     tbuf[0, FEAT:DEEP, 0:HALF] = extra(parts, 3)
     pl.semaphore_wait(barrier, len(NEAR))
+    for dz in (1, 7):
+        pl.semaphore_signal(ready1, inc=1, device_id=device(dz=dz), device_id_type=MESH)
     forward((0, 0), 0)
     for t in (1, 2):
         begin(("t", t), functools.partial(target_copy, t))
     forward((0, 0), 1)
     fetches[4].wait()
     acc[...] = jnp.zeros_like(acc)
+    pl.semaphore_wait(ready1, 2)
+    for dz in (2, 6):
+        pl.semaphore_signal(ready2, inc=1, device_id=device(dz=dz), device_id_type=MESH)
 
     def block(sources, targets):
         cross = lax.dot_general(
@@ -212,93 +222,78 @@
         return jnp.concatenate([sbuf[g, 0], sbuf[g, 1]], axis=1)
 
     def quarter_of(t):
-        return tbuf[t // 2, :, pl.ds(pl.multiple_of(t % 2 * HALF, HALF), HALF)]
-
-    def events(step, table):
-        for at, action in table.items():
-            pl.when(step == at)(action)
-
-    def part_here(part):
+        return tbuf[t // 2, :, pl.ds(t % 2 * HALF if isinstance(t, int) else pl.multiple_of(t % 2 * HALF, HALF), HALF)]
+
+    def target_here(t):
+        target_copy(t).wait_recv()
+        begin(("t", t + 2), functools.partial(target_relay, t))
+
+    def far():
+        pl.semaphore_wait(ready2, 2)
+        begin(("ring", (4, 0), None), functools.partial(ring, (0, 0), (4, 0), None, opposite))
+
+    def at(step):
         def action():
-            for piece in ((-1, 0), (1, 0), (0, 1)):
-                arrive(piece, part)
-            from_core(0, part)
-            from_core(1, part)
+            for pieces, part in ARRIVE.get(step, ()):
+                for piece in pieces:
+                    arrive(piece, part)
+            for pair, part in CORE.get(step, ()):
+                from_core(pair, part)
+            for t in TARGET.get(step, ()):
+                target_here(t)
+            if step == FAR:
+                far()
         return action
 
-    def begins(part, carry):
-        events(part, {0: part_here(0), 1: part_here(1)})
+    def events(index, first, count):
+        for n in range(count):
+            if first + n in ARRIVE or first + n in CORE or first + n in TARGET or first + n == FAR:
+                if isinstance(index, int):
+                    if index == n:
+                        at(first + n)()
+                else:
+                    pl.when(index == n)(at(first + n))
+
+    def own_targets(part, carry):
+        events(part, 0, 2)
         acc[0] += block(jnp.concatenate([sbuf[0, part], sbuf[1, part]], axis=1), tbuf[0, :, 0:HALF])
         return carry
 
-    lax.fori_loop(0, 2, begins, 0)
-
-    def target_here(t):
-        def action():
-            target_copy(t).wait_recv()
-            begin(("t", t + 2), functools.partial(target_relay, t))
-        return action
-
-    def second():
-        for piece in ((-2, 0), (2, 0)):
-            arrive(piece)
-
-    def first(m, carry):
-        events(m, {0: target_here(1), 2: target_here(2), 3: second})
+    for n in range(2):
+        own_targets(n, 0)
+
+    def next_targets(m, carry):
+        events(m, 2, 4)
         t = 1 + m // 2
         acc[t] += block(pair_of(m % 2), quarter_of(t))
         return carry
 
-    lax.fori_loop(0, 4, first, 0)
-
-    def at0():
-        from_core(2)
-
-    def at1():
-        arrive((-1, 1))
-        arrive((1, 1))
-        for t in (1, 2):
-            target_relay(t).wait_recv()
-        for g in (0, 1):
-            acc[3] += block(pair_of(g), tbuf[1, :, HALF:])
-
-    def at2():
-        arrive((3, 0))
-        arrive((-3, 0))
-        arrive((2, 1))
-        from_core(3)
-
-    def at4():
-        arrive((-2, 1))
-        from_core(4)
-
-    def at6():
-        arrive((3, 1))
-        from_core(5)
-
-    def at9():
-        arrive((-3, 1))
-        arrive((4, 1))
+    for n in range(4):
+        next_targets(n, 0)
 
     def middle(n, carry):
-        events(n, {
-            0: at0,
-            1: at1,
-            2: at2,
-            4: at4,
-            6: at6,
-            7: lambda: arrive((4, 0)),
-            8: lambda: from_core(6),
-            9: at9,
-        })
+        events(n, 6, 10)
+
+        def extra_block():
+            for t in (1, 2):
+                target_relay(t).wait_recv()
+            for g in (0, 1):
+                acc[3] += block(pair_of(g), tbuf[1, :, HALF:])
+
+        if isinstance(n, int):
+            if n == 1:
+                extra_block()
+        else:
+            pl.when(n == 1)(extra_block)
         h = n % 2
         part = block(pair_of(2 + n // 2), tbuf[h])
         acc[2 * h] += part[:, 0:HALF]
         acc[2 * h + 1] += part[:, HALF:]
         return carry
 
-    lax.fori_loop(0, 10, middle, 0)
-    from_core(7)
+    for n in range(10):
+        middle(n, 0)
+    at(16)()
 
     mine = x * 2 + yl
 
@@ -316,10 +311,15 @@
     def last(n, carry):
         t = 3 - n
         parting[t] = (acc[t] + block(pair_of(7), quarter_of(t))).astype(BF16)
-        events(t, {s: leave(s) for s in (3, 2, 1, 0)})
+        if isinstance(t, int):
+            leave(t)()
+        else:
+            for s in (3, 2, 1, 0):
+                pl.when(t == s)(leave(s))
         return carry
 
-    lax.fori_loop(0, 4, last, 0)
+    for n in range(4):
+        last(n, 0)
     reduced[mine] = parting[0]
     rhs = probes_ref[:, pl.ds(half_at, HALF)]
     diagonal = noise_ref[:, pl.ds(half_at, HALF)] * rhs
@@ -343,25 +343,19 @@
     spread = jnp.zeros((PROBES, 128), F32)
     for n, column in enumerate((norm, curve, square)):
         spread = jnp.where(lane == probe + PROBES * n, column, spread)
-    rows[pl.ds(c, 1), :] = jnp.sum(spread, axis=0, keepdims=True)
-
-    def row_copy(at):
-        return copy(rows.at[pl.ds(at, 1)], rows.at[pl.ds(at, 1)], row_send.at[0], row_recv.at[0], sibling)
-
-    begin("row", functools.partial(row_copy, c))
+    here = pl.ds(loop * 2 + c, 1)
+    sums[here, :] = jnp.sum(spread, axis=0, keepdims=True)
+    for dx, dy, dz, dc in PEERS:
+        copy(
+            sums.at[here], sums.at[here], sum_send.at[0], sum_recv.at[0],
+            device(dx=dx, dh=dy, dl=dy, dz=dz, dc=dc),
+        ).start()
     span = pl.ds(half_at, HALF)
     image_ref[:, span] = image
 
     def image_copy(at):
         return copy(image_ref.at[:, at], image_ref.at[:, at], i_send.at[0], i_recv.at[0], sibling)
 
-    row_copy(1 - c).wait_recv()
-    sums[pl.ds(loop, 1), :] = rows[0:1, :] + rows[1:2, :]
-    for dx, dy, dz in PEERS:
-        copy(
-            sums.at[pl.ds(loop, 1)], sums.at[pl.ds(loop, 1)], sum_send.at[0], sum_recv.at[0],
-            device(dx=dx, dh=dy, dl=dy, dz=dz),
-        ).start()
     begin("image", functools.partial(image_copy, span))
     image_copy(pl.ds(pl.multiple_of((1 - c) * HALF, HALF), HALF)).wait_recv()
     for make in started.values():
@@ -403,11 +397,11 @@
             pltpu.VMEM((4, PROBES, HALF), F32),
             pltpu.VMEM((4, PROBES, HALF), BF16),
             pltpu.VMEM((8, PROBES, HALF), BF16),
-            pltpu.VMEM((8, 128), F32),
-            pltpu.VMEM((64, 128), F32),
+            pltpu.VMEM((128, 128), F32),
             dma((5,)),
-            dma((8, 2, 2)), dma((8, 2, 2)), dma((5,)), dma((4, 2)), dma((1,)), dma((1,)), dma((1,)),
-            dma((8, 2, 2)), dma((8, 2, 2)), dma((5,)), dma((8,)), dma((1,)), dma((1,)), dma((1,)),
+            dma((8, 2, 2)), dma((8, 2, 2)), dma((5,)), dma((4, 2)), dma((1,)), dma((1,)),
+            dma((8, 2, 2)), dma((8, 2, 2)), dma((5,)), dma((8,)), dma((1,)), dma((1,)),
+            pltpu.SemaphoreType.REGULAR, pltpu.SemaphoreType.REGULAR,
         ],
         compiler_params=pltpu.CompilerParams(
             collective_id=0, has_side_effects=True, vmem_limit_bytes=56 << 20

time: 47.9 us -> 47.4 us (0.990)
  Pallas kernels: 46.5 us -> 46 us
    pallas_call x1, Pallas kernels: 46.5 us -> 46 us  [local(): pl.pallas_call(kernel, out_shape=(shape, shape, shape), in_specs=[pl.Bloc...]
where the time goes in v4:
time: 47.4 us; the launch traced here: 47.3 us
  Pallas kernels  46 us (97%)
  other arithmetic  0.69 us (1%)
  between operations  0.66 us (1%)
    pallas_call x1, Pallas kernels, local(): pl.pallas_call(kernel, out_shape=(shape, shape, shape), in_specs=[pl.Bloc...  46 us

profile of v4, /device:TPU:1, one launch (start us, length us, event | category | flops | bytes accessed | tf_op | source)
XLA Modules:
  0.0 47.3 jit_solution(835926950429501409)
XLA Ops:
  0.6 0.0 copy-start
  0.6 46.0 %cg_step.1 = (f32[16,1024]{1,0:T(8,128)S(1)}, f32[16,1024]{1,0:T(8,128)S(1)}, f32[16,1024]{1,0:T(8,128)S(1)}) custom-call(bf16[1024,128]{1,0:T(8,128)(2,1)} %desc_hbm.1, f32[1,128]{1,0:T(1,128)} %bitcast.3, f32[1,1024]{1,0:T(1,128)} %bitcast.2, f32[16,1024]{1,0:T(8,128)} %probes_hbm.1), custom_call_target="tpu_custom_call" | custom-call | flops 5000000000 | bytes 1000000 | tf_op jit(solution)/shard_map/cg_step/pallas_call | solution.py:384
  46.6 0.0 copy-done
  46.6 0.7 %multiply_add_fusion = (f32[16,1024]{1,0:T(8,128)}, f32[16,1024]{1,0:T(8,128)}, f32[16,1024]{1,0:T(8,128)}) fusion(f32[16,1024]{1,0:T(8,128)S(1)} %get-tuple-element.8, f32[16,1024]{1,0:T(8,128)S(1)} %copy-done, f32[16,1024]{1,0:T(8,128)S(1)} %get-tuple-element.6, f32[16,1024]{1,0:T(8,128)S(1)} %get-tuple-element.7), kind=kLoop, calls=%fused_computation | loop fusion | flops 81920 | bytes 458752 | tf_op jit(solution)/shard_map/add | solution.py:413
Async XLA Ops:
  0.6 46.0 %copy-start = (f32[16,1024]{1,0:T(8,128)S(1)}, f32[16,1024]{1,0:T(8,128)}, u32[]{:S(2)}) copy-start(f32[16,1024]{1,0:T(8,128)} %probes_hbm.1) | copy-start | bytes 196612

commit v5 on v4

--- a/solution.py
+++ b/solution.py
@@ -31,16 +31,15 @@
     ((-2, 1), (3, 1)),
     ((4, 1), (-3, 1)),
 )
-SPLIT = 4
 PLACE = {piece: (g, i) for g, pair in enumerate(PAIRS) for i, piece in enumerate(pair)}
 UP = {(0, 0): (-1, 0), (-1, 0): (-2, 0), (-2, 0): (-3, 0), (-2, 1): (-3, 1)}
 DOWN = {(0, 0): (1, 0), (1, 0): (2, 0), (2, 0): (3, 0), (2, 1): (3, 1)}
 ACROSS = {(0, 0): (0, 1), (-1, 0): (-1, 1), (1, 0): (1, 1), (-2, 0): (-2, 1), (2, 0): (2, 1), (4, 0): (4, 1)}
 NEXT = ((-1, 0), (1, 0), (0, 1))
-ARRIVE = {0: ((((-1, 0), (1, 0), (0, 1)), 0),), 1: ((((-1, 0), (1, 0), (0, 1)), 1),), 6: ((((-2, 0), (2, 0)), None),), 7: ((((-1, 1), (1, 1)), None),), 8: ((((2, 1), (4, 0)), None),), 9: ((((3, 0), (-3, 0)), None),), 10: ((((-2, 1),), None),), 13: ((((3, 1),), None),), 14: ((((4, 1),), None),), 15: ((((-3, 1),), None),)}
+ARRIVE = {0: ((((-1, 0), (1, 0), (0, 1)), 0),), 1: ((((-1, 0), (1, 0), (0, 1)), 1),), 4: ((((-2, 0), (2, 0)), 0),), 5: ((((-2, 0), (2, 0)), 1),), 6: ((((-1, 1), (1, 1)), 0),), 7: ((((-1, 1), (1, 1)), 1),), 8: ((((2, 1), (-2, 1)), 0), (((3, 0), (-3, 0)), 0)), 9: ((((2, 1), (-2, 1)), 1), (((3, 0), (-3, 0)), 1), (((4, 0),), None)), 11: ((((3, 1),), 0),), 12: ((((-3, 1),), 0), (((3, 1),), 1)), 13: ((((-3, 1),), 1),), 14: ((((4, 1),), None),)}
 CORE = {0: ((0, 0), (1, 0)), 1: ((0, 1), (1, 1)), 6: ((2, None),), 8: ((3, None),), 10: ((4, None),), 12: ((5, None),), 14: ((6, None),), 16: ((7, None),)}
 TARGET = {2: (1,), 4: (2,)}
-FAR = 2
+FAR = 3
 TARGET_X = (0, 1, 3, 2)
 NEAR = (
     (0, 0, 0, 1, 0), (0, 0, 0, 7, 0), (0, 1, 1, 0, 0), (0, 0, 0, 0, 1), (0, 0, 1, 0, 0),
@@ -116,11 +115,7 @@
 
     def place(piece, core, part):
         g, i = PLACE[piece]
-        points = pl.ds(pl.multiple_of(i * QUART + core * PART, PART), PART)
-        return sbuf.at[g, :, :, points] if part is None else sbuf.at[g, part, :, points]
-
-    def parts_of(piece):
-        return (0, 1) if PLACE[piece][0] < SPLIT else (None,)
+        return sbuf.at[g, part, :, pl.ds(pl.multiple_of(i * QUART + core * PART, PART), PART)]
 
     started = {}
 
@@ -134,41 +129,31 @@
         )
 
     def ring(src, dst, part, to):
-        at = PLACE[dst] + (part or 0,)
+        at = PLACE[dst] + (part,)
         return copy(place(src, c, part), place(dst, c, part), ring_send.at[at], ring_recv.at[at], to)
 
     ways = ((UP, device(dz=1)), (DOWN, device(dz=7)), (ACROSS, device(dh=1, dl=1)))
     sibling, opposite = device(dc=1), device(dz=4)
 
     def core_copy(piece, part, core):
-        at = PLACE[piece] + (part or 0,)
+        at = PLACE[piece] + (part,)
         return copy(place(piece, core, part), place(piece, core, part), core_send.at[at], core_recv.at[at], sibling)
 
-    def from_core(pair, part=None):
-        for piece in PAIRS[pair]:
-            for p in parts_of(piece):
-                if part is None or p == part:
-                    core_copy(piece, p, 1 - c).wait_recv()
+    def from_core(pair, part):
+        for p in (0, 1) if part is None else (part,):
+            for piece in PAIRS[pair]:
+                core_copy(piece, p, 1 - c).wait_recv()
 
     def forward(piece, part):
         for table, to in ways:
             if piece in table:
-                onward = table[piece]
-                for p in parts_of(onward) if part is None else (part,):
-                    begin(("ring", onward, p), functools.partial(ring, piece, onward, p, to))
+                begin(("ring", table[piece], part), functools.partial(ring, piece, table[piece], part, to))
         begin(("core", piece, part), functools.partial(core_copy, piece, part, c))
 
-    def arrive(piece, part=None):
-        for p in parts_of(piece) if part is None else (part,):
+    def arrive(piece, part):
+        for p in (0, 1) if part is None else (part,):
             ring(piece, piece, p, ways[0][1]).wait_recv()
-        if part is None and parts_of(piece) == (0, 1):
-            for table, to in ways:
-                if piece in table:
-                    begin(("ring", table[piece], None), functools.partial(ring, piece, table[piece], None, to))
-            for p in (0, 1):
-                begin(("core", piece, p), functools.partial(core_copy, piece, p, c))
-        else:
-            forward(piece, part)
+            forward(piece, p)
 
     def target(t, first=0, count=HALF):
         return tbuf.at[t // 2, :, pl.ds(t % 2 * HALF + first, count)]
@@ -230,7 +215,8 @@
 
     def far():
         pl.semaphore_wait(ready2, 2)
-        begin(("ring", (4, 0), None), functools.partial(ring, (0, 0), (4, 0), None, opposite))
+        for p in (0, 1):
+            begin(("ring", (4, 0), p), functools.partial(ring, (0, 0), (4, 0), p, opposite))
 
     def at(step):
         def action():
@@ -279,6 +265,7 @@
                 target_relay(t).wait_recv()
             for g in (0, 1):
                 acc[3] += block(pair_of(g), tbuf[1, :, HALF:])
+            at(17)()
 
         if isinstance(n, int):
             if n == 1:

time: 47.4 us -> 45.8 us (0.966)
  Pallas kernels: 46 us -> 44.3 us
    pallas_call x1, Pallas kernels: 46 us -> 44.3 us  [local(): pl.pallas_call(kernel, out_shape=(shape, shape, shape), in_specs=[pl.Bloc...]
where the time goes in v5:
time: 45.8 us; the launch traced here: 45.7 us
  Pallas kernels  44.3 us (97%)
  other arithmetic  0.69 us (2%)
  between operations  0.66 us (1%)
    pallas_call x1, Pallas kernels, local(): pl.pallas_call(kernel, out_shape=(shape, shape, shape), in_specs=[pl.Bloc...  44.3 us

profile of v5, /device:TPU:1, one launch (start us, length us, event | category | flops | bytes accessed | tf_op | source)
XLA Modules:
  0.0 45.7 jit_solution(6975134265374072876)
XLA Ops:
  0.6 0.0 copy-start
  0.6 44.3 %cg_step.1 = (f32[16,1024]{1,0:T(8,128)S(1)}, f32[16,1024]{1,0:T(8,128)S(1)}, f32[16,1024]{1,0:T(8,128)S(1)}) custom-call(bf16[1024,128]{1,0:T(8,128)(2,1)} %desc_hbm.1, f32[1,128]{1,0:T(1,128)} %bitcast.3, f32[1,1024]{1,0:T(1,128)} %bitcast.2, f32[16,1024]{1,0:T(8,128)} %probes_hbm.1), custom_call_target="tpu_custom_call" | custom-call | flops 5000000000 | bytes 1000000 | tf_op jit(solution)/shard_map/cg_step/pallas_call | solution.py:371
  45.0 0.0 copy-done
  45.0 0.7 %multiply_add_fusion = (f32[16,1024]{1,0:T(8,128)}, f32[16,1024]{1,0:T(8,128)}, f32[16,1024]{1,0:T(8,128)}) fusion(f32[16,1024]{1,0:T(8,128)S(1)} %get-tuple-element.8, f32[16,1024]{1,0:T(8,128)S(1)} %copy-done, f32[16,1024]{1,0:T(8,128)S(1)} %get-tuple-element.6, f32[16,1024]{1,0:T(8,128)S(1)} %get-tuple-element.7), kind=kLoop, calls=%fused_computation | loop fusion | flops 81920 | bytes 458752 | tf_op jit(solution)/shard_map/add | solution.py:400
Async XLA Ops:
  0.6 44.3 %copy-start = (f32[16,1024]{1,0:T(8,128)S(1)}, f32[16,1024]{1,0:T(8,128)}, u32[]{:S(2)}) copy-start(f32[16,1024]{1,0:T(8,128)} %probes_hbm.1) | copy-start | bytes 196612

commit v6 on v5

--- a/solution.py
+++ b/solution.py
@@ -263,8 +263,8 @@
         def extra_block():
             for t in (1, 2):
                 target_relay(t).wait_recv()
-            for g in (0, 1):
-                acc[3] += block(pair_of(g), tbuf[1, :, HALF:])
+            both = jnp.concatenate([pair_of(0), pair_of(1)], axis=1)
+            acc[3] += block(both, tbuf[1, :, HALF:])
             at(17)()
 
         if isinstance(n, int):
@@ -305,7 +305,11 @@
                 pl.when(t == s)(leave(s))
         return carry
 
-    for n in range(4):
+    part = block(pair_of(7), tbuf[1])
+    for t in (3, 2):
+        parting[t] = (acc[t] + part[:, (t - 2) * HALF:(t - 1) * HALF]).astype(BF16)
+        leave(t)()
+    for n in (2, 3):
         last(n, 0)
     reduced[mine] = parting[0]
     rhs = probes_ref[:, pl.ds(half_at, HALF)]

time: 45.8 us -> 46 us (level)
  no operation moved by 1% of the time
where the time goes in v6:
time: 46 us; the launch traced here: 45.9 us
  Pallas kernels  44.5 us (97%)
  other arithmetic  0.69 us (2%)
  between operations  0.66 us (1%)
    pallas_call x1, Pallas kernels, local(): pl.pallas_call(kernel, out_shape=(shape, shape, shape), in_specs=[pl.Bloc...  44.5 us

profile of v6, /device:TPU:1, one launch (start us, length us, event | category | flops | bytes accessed | tf_op | source)
XLA Modules:
  0.0 45.9 jit_solution(13243929593746697928)
XLA Ops:
  0.6 0.0 copy-start
  0.6 44.5 %cg_step.1 = (f32[16,1024]{1,0:T(8,128)S(1)}, f32[16,1024]{1,0:T(8,128)S(1)}, f32[16,1024]{1,0:T(8,128)S(1)}) custom-call(bf16[1024,128]{1,0:T(8,128)(2,1)} %desc_hbm.1, f32[1,128]{1,0:T(1,128)} %bitcast.3, f32[1,1024]{1,0:T(1,128)} %bitcast.2, f32[16,1024]{1,0:T(8,128)} %probes_hbm.1), custom_call_target="tpu_custom_call" | custom-call | flops 5000000000 | bytes 1000000 | tf_op jit(solution)/shard_map/cg_step/pallas_call | solution.py:375
  45.2 0.0 copy-done
  45.2 0.7 %multiply_add_fusion = (f32[16,1024]{1,0:T(8,128)}, f32[16,1024]{1,0:T(8,128)}, f32[16,1024]{1,0:T(8,128)}) fusion(f32[16,1024]{1,0:T(8,128)S(1)} %get-tuple-element.8, f32[16,1024]{1,0:T(8,128)S(1)} %copy-done, f32[16,1024]{1,0:T(8,128)S(1)} %get-tuple-element.6, f32[16,1024]{1,0:T(8,128)S(1)} %get-tuple-element.7), kind=kLoop, calls=%fused_computation | loop fusion | flops 81920 | bytes 458752 | tf_op jit(solution)/shard_map/add | solution.py:404
Async XLA Ops:
  0.6 44.5 %copy-start = (f32[16,1024]{1,0:T(8,128)S(1)}, f32[16,1024]{1,0:T(8,128)}, u32[]{:S(2)}) copy-start(f32[16,1024]{1,0:T(8,128)} %probes_hbm.1) | copy-start | bytes 196612
